TPU v7x, 32 devices: a whole 2x2x4 slice. The times are simulated.
32 devices in a mesh: parts: 2 (over y), row: 8 (over z, x), col: 2 (over core).
Axes of the slice: x: 2, y: 2, z: 4, core: 2. Of those that a mesh axis runs over, the one named last changes fastest.
Arguments:
- right_sides: float32 [16384, 2048], P(('parts', 'row'), 'col'), parts along dimension 0, may hold values from -6 to 6
- lower_panel: float32 [16384, 1024], P(('parts', 'row')), parts along dimension 0, as said below
- upper_panel: float32 [16384, 1024], P(('parts', 'row')), parts along dimension 0, as said below
Outputs:
- solution: float32 [16384, 2048], P(('parts', 'row'), 'col'), parts along dimension 0
There are 2 independent parts, one for each index of `parts`. A program takes and returns all parts, laid end to end along the dimension named above; each array names one. Nothing has to cross between parts.
Inputs may be any that keep to these rules, and one draw needn't show every extreme that they name: `lower_panel`: column block k (columns k*256 to (k+1)*256 - 1) is zero in rows above k*256; its rows k*256 to (k+1)*256 - 1 form a unit lower triangular block. `upper_panel`: with b = 28 + j, column block j is zero in rows from (b+1)*256 on; its rows b*256 to (b+1)*256 - 1 form an upper triangular block whose diagonal entries have magnitudes from 1 to 2.
All inputs are finite; a program needn't handle non-finite values.
Results may differ from a plain program's by a relative error of at most 0.00013.
Values sent between devices are 32-bit elements; how exact they have to be, the bound alone decides.
A program may use at most 128 MiB of HBM per device.

v0:
```python
import jax
import jax.numpy as jnp
from jax import lax
from jax.sharding import PartitionSpec as P

NB = 256
KB = 4


def broadcast(value, axis, source):
    kept = jnp.where(lax.axis_index(axis) == source, value, 0).astype(value.dtype)
    return lax.psum(kept, axis)


def small_inverse(matrix, forward):
    precise = lax.Precision.HIGHEST
    order = matrix.shape[0]
    rows = lax.iota(jnp.int32, order)[:, None]
    columns = lax.iota(jnp.int32, order)[None, :]
    ident = jnp.where(rows == columns, 1.0, 0.0).astype(jnp.float32)
    if forward:
        strict = jnp.where(rows > columns, matrix, 0.0)
        scaling = jnp.ones((order,), jnp.float32)
    else:
        scaling = 1.0 / jnp.sum(jnp.where(rows == columns, matrix, 0.0), axis=1)
        strict = scaling[:, None] * jnp.where(rows < columns, matrix, 0.0)
    power = -strict
    result = ident + power
    reach = 2
    while reach < order:
        power = jnp.dot(power, power, precision=precise)
        result = jnp.dot(result, ident + power, precision=precise)
        reach = reach * 2
    return result * scaling[None, :]


def block_solve(matrix, values, forward):
    precise = lax.Precision.HIGHEST
    order = matrix.shape[0]
    if order <= 16:
        return jnp.dot(small_inverse(matrix, forward), values, precision=precise)
    half = order // 2
    if forward:
        upper_part = block_solve(matrix[:half, :half], values[:half], True)
        rest = values[half:] - jnp.dot(matrix[half:, :half], upper_part, precision=precise)
        lower_part = block_solve(matrix[half:, half:], rest, True)
    else:
        lower_part = block_solve(matrix[half:, half:], values[half:], False)
        rest = values[:half] - jnp.dot(matrix[:half, half:], lower_part, precision=precise)
        upper_part = block_solve(matrix[:half, :half], rest, False)
    return jnp.concatenate([upper_part, lower_part], axis=0)


def make_groups(order, local_rows):
    groups = []
    for column, block_index in order:
        owner_row = block_index * NB // local_rows
        groups.append((owner_row, [(column, block_index)]))
    return groups


def solve_members(current, factor_panel, members, owner_row, local_rows, forward):
    precise = lax.Precision.HIGHEST
    solved = []
    for position in range(len(members)):
        column, block_index = members[position]
        offset = block_index * NB - owner_row * local_rows
        target = current[offset : offset + NB]
        for earlier in range(position):
            prior_column = members[earlier][0]
            coupling = factor_panel[
                offset : offset + NB, prior_column * NB : (prior_column + 1) * NB
            ]
            target = target - jnp.dot(coupling, solved[earlier], precision=precise)
        diagonal_block = factor_panel[offset : offset + NB, column * NB : (column + 1) * NB]
        solved.append(block_solve(diagonal_block, target, forward))
    return jnp.concatenate(solved, axis=0)


def run_sweep(current, factor_panel, groups, forward, row_index, send_rows):
    precise = lax.Precision.HIGHEST
    local_rows = current.shape[0]
    global_rows = row_index * local_rows + lax.iota(jnp.int32, local_rows)
    for owner_row, members in groups:

        def solve_here():
            return solve_members(current, factor_panel, members, owner_row, local_rows, forward)

        def nothing():
            return jnp.zeros((len(members) * NB, current.shape[1]), jnp.float32)

        stacked = lax.cond(row_index == owner_row, solve_here, nothing)
        stacked = send_rows(stacked, owner_row)
        masked_columns = []
        for column, block_index in members:
            column_piece = factor_panel[:, column * NB : (column + 1) * NB]
            if forward:
                keep_rows = global_rows >= (block_index + 1) * NB
            else:
                keep_rows = global_rows < block_index * NB
            masked_columns.append(jnp.where(keep_rows[:, None], column_piece, 0.0))
        current = current - jnp.dot(
            jnp.concatenate(masked_columns, axis=1), stacked, precision=precise
        )
        inside = row_index == owner_row
        for position in range(len(members)):
            offset = members[position][1] * NB - owner_row * local_rows
            rows_now = current[offset : offset + NB]
            fresh = stacked[position * NB : (position + 1) * NB]
            current = current.at[offset : offset + NB].set(jnp.where(inside, fresh, rows_now))
    return current


def shards(right_sides, lower_panel, upper_panel):
    local_rows = right_sides.shape[0]
    row_index = lax.axis_index("row")
    total_blocks = lax.axis_size("row") * local_rows // NB

    def send_lower(values, root):
        return jax.tree.map(lambda part: broadcast(part, "row", root), values)

    def send_upper(values, root):
        return jax.tree.map(lambda part: broadcast(part, "row", root), values)

    forward_order = [(column, column) for column in range(KB)]
    backward_order = [(column, total_blocks - KB + column) for column in range(KB - 1, -1, -1)]
    current = right_sides.astype(jnp.float32)
    current = run_sweep(
        current, lower_panel, make_groups(forward_order, local_rows), True, row_index, send_lower
    )
    current = run_sweep(
        current, upper_panel, make_groups(backward_order, local_rows), False, row_index, send_upper
    )
    return current


def solution(mesh):
    placed = (P(("parts", "row"), "col"), P(("parts", "row"), None), P(("parts", "row"), None))
    return jax.shard_map(
        shards, mesh=mesh, in_specs=placed, out_specs=P(("parts", "row"), "col"), check_vma=False
    )
```

profile of v0, /device:TPU:2, one launch (start us, length us, event | category | flops | bytes accessed | tf_op | source)
XLA Modules:
  0.0 1270.0 jit_solution(15444185294185869671)
XLA Ops:
  6.5 1.1 conditional.8
  6.5 1.1 broadcast.685
  7.6 1.1 broadcast_select_fusion.7
  8.7 0.0 all-reduce.9.cloned.1.call-update
  8.7 0.0 all-reduce.11.cloned.1.call-start
  8.8 144.4 %all-reduce.9.cloned.1.call-done = f32[256,1024]{1,0:T(8,128)} async-done(((f32[256,1024]{1,0:T(8,128)}), f32[256,1024]{1,0:T(8,128)}) %all-reduce.9.cloned.1.call-update) | async-done | bytes 1048592 | tf_op jit(solution)/shard_map/psum | solution.py:12
  153.2 6.8 convolution_subtract_fusion.7
  159.9 0.3 fusion.2423
  160.2 2.0 copy-done.6
  162.2 1.6 conditional.9
  162.2 1.2 broadcast.686
  163.8 1.1 broadcast_select_fusion.6
  165.0 0.0 all-reduce.11.cloned.1.call-update
  165.0 0.0 all-reduce.13.cloned.1.call-start
  165.0 142.4 %all-reduce.11.cloned.1.call-done = f32[256,1024]{1,0:T(8,128)} async-done(((f32[256,1024]{1,0:T(8,128)}), f32[256,1024]{1,0:T(8,128)}) %all-reduce.11.cloned.1.call-update) | async-done | bytes 1048592 | tf_op jit(solution)/shard_map/psum | solution.py:12
  307.5 6.8 convolution_subtract_fusion.6
  314.2 0.3 fusion.2422
  314.5 2.0 copy-done.1
  316.5 1.3 conditional.10
  316.5 1.2 broadcast.687
  317.9 1.1 broadcast_select_fusion.5
  319.0 0.0 all-reduce.15.cloned.1.call-start
  319.1 142.6 %all-reduce.13.cloned.1.call-done = f32[256,1024]{1,0:T(8,128)} async-done(((f32[256,1024]{1,0:T(8,128)}), f32[256,1024]{1,0:T(8,128)}) %all-reduce.13.cloned.1.call-update) | async-done | bytes 1048592 | tf_op jit(solution)/shard_map/psum | solution.py:12
  461.7 6.8 convolution_subtract_fusion.5
  468.4 0.3 fusion.2421
  468.7 2.0 copy-done.2
  470.7 1.3 conditional.11
  470.7 1.2 broadcast.688
  472.1 1.1 broadcast_select_fusion.4
  473.2 0.0 all-reduce.17.cloned.1.call-start
  473.3 142.7 %all-reduce.15.cloned.1.call-done = f32[256,1024]{1,0:T(8,128)} async-done(((f32[256,1024]{1,0:T(8,128)}), f32[256,1024]{1,0:T(8,128)}) %all-reduce.15.cloned.1.call-update) | async-done | bytes 1048592 | tf_op jit(solution)/shard_map/psum | solution.py:12
  616.0 6.8 convolution_subtract_fusion.4
  622.8 0.3 fusion.2420
  623.1 2.0 copy-done
  625.1 1.5 conditional.12
  625.1 1.2 broadcast.689
  626.6 1.1 broadcast_select_fusion.3
  627.8 0.0 all-reduce.19.cloned.1.call-start
  627.8 147.3 %all-reduce.17.cloned.1.call-done = f32[256,1024]{1,0:T(8,128)} async-done(((f32[256,1024]{1,0:T(8,128)}), f32[256,1024]{1,0:T(8,128)}) %all-reduce.17.cloned.1.call-update) | async-done | bytes 1048592 | tf_op jit(solution)/shard_map/psum | solution.py:12
  775.1 6.8 convolution_subtract_fusion.3
  781.9 0.3 fusion.2419
  782.2 2.0 copy-done.3
  784.2 1.3 conditional.13
  784.2 1.2 broadcast.691
  785.5 1.1 broadcast_select_fusion.2
  786.6 0.0 all-reduce.21.cloned.1.call-start
  786.7 147.2 %all-reduce.19.cloned.1.call-done = f32[256,1024]{1,0:T(8,128)} async-done(((f32[256,1024]{1,0:T(8,128)}), f32[256,1024]{1,0:T(8,128)}) %all-reduce.19.cloned.1.call-update) | async-done | bytes 1048592 | tf_op jit(solution)/shard_map/psum | solution.py:12
  933.9 6.8 convolution_subtract_fusion.2
  940.7 0.3 fusion.2418
  941.0 2.0 copy-done.4
  943.0 1.3 conditional.14
  943.0 1.2 broadcast.693
  944.3 1.1 broadcast_select_fusion.1
  945.5 0.0 all-reduce.23.cloned.1.call-start
  945.5 147.2 %all-reduce.21.cloned.1.call-done = f32[256,1024]{1,0:T(8,128)} async-done(((f32[256,1024]{1,0:T(8,128)}), f32[256,1024]{1,0:T(8,128)}) %all-reduce.21.cloned.1.call-update) | async-done | bytes 1048592 | tf_op jit(solution)/shard_map/psum | solution.py:12
  1092.7 6.8 convolution_subtract_fusion.1
  1099.5 0.3 fusion.2417
  1099.8 2.0 copy-done.5
  1101.8 1.4 conditional.15
  1101.8 1.2 broadcast.695
  1103.2 1.1 broadcast_select_fusion
  1104.4 147.5 %all-reduce.23.cloned.1.call-done = f32[256,1024]{1,0:T(8,128)} async-done(((f32[256,1024]{1,0:T(8,128)}), f32[256,1024]{1,0:T(8,128)}) %all-reduce.23.cloned.1.call-update) | async-done | bytes 1048592 | tf_op jit(solution)/shard_map/psum | solution.py:12
  1251.9 8.4 convolution_subtract_fusion
  1260.3 2.4 fusion.2416
  (38 shorter events, 0.2 us)
Async XLA Ops:
  6.5 146.6 %all-reduce.9.cloned.1.call-start = ((), (), s32[]{:S(2)}) async-start(), calls=%async_computation | async-start | bytes 2097152 | tf_op jit(solution)/shard_map/psum | solution.py:12
  8.7 298.7 %all-reduce.11.cloned.1.call-start = ((), (), s32[]{:S(2)}) async-start(), calls=%async_computation.1 | async-start | bytes 2097152 | tf_op jit(solution)/shard_map/psum | solution.py:12
  153.2 6.8 copy-start.8
  160.2 2.0 copy-start.6
  165.0 296.7 %all-reduce.13.cloned.1.call-start = ((), (), s32[]{:S(2)}) async-start(), calls=%async_computation.2 | async-start | bytes 2097152 | tf_op jit(solution)/shard_map/psum | solution.py:12
  307.5 6.8 copy-start.9
  314.5 2.0 copy-start.1
  319.0 297.0 %all-reduce.15.cloned.1.call-start = ((), (), s32[]{:S(2)}) async-start(), calls=%async_computation.3 | async-start | bytes 2097152 | tf_op jit(solution)/shard_map/psum | solution.py:12
  461.7 6.8 copy-start.10
  468.7 2.0 copy-start.2
  473.2 301.9 %all-reduce.17.cloned.1.call-start = ((), (), s32[]{:S(2)}) async-start(), calls=%async_computation.4 | async-start | bytes 2097152 | tf_op jit(solution)/shard_map/psum | solution.py:12
  616.0 6.8 copy-start.7
  623.1 2.0 copy-start
  627.8 306.1 %all-reduce.19.cloned.1.call-start = ((), (), s32[]{:S(2)}) async-start(), calls=%async_computation.5 | async-start | bytes 2097152 | tf_op jit(solution)/shard_map/psum | solution.py:12
  775.1 6.8 copy-start.11
  782.2 2.0 copy-start.3
  786.6 306.1 %all-reduce.21.cloned.1.call-start = ((), (), s32[]{:S(2)}) async-start(), calls=%async_computation.6 | async-start | bytes 2097152 | tf_op jit(solution)/shard_map/psum | solution.py:12
  933.9 6.8 copy-start.12
  940.9 2.0 copy-start.4
  945.5 306.4 %all-reduce.23.cloned.1.call-start = ((), (), s32[]{:S(2)}) async-start(), calls=%async_computation.7 | async-start | bytes 2097152 | tf_op jit(solution)/shard_map/psum | solution.py:12
  1092.7 6.8 copy-start.13
  1099.8 2.0 copy-start.5
  1251.9 8.4 copy-start.14
Sparse Core Ops, SparseCore 0:
  10.9 142.2 all-reduce.8
  165.1 142.3 all-reduce.10
  319.1 142.5 all-reduce.12
  473.4 142.6 all-reduce.14
  627.9 147.1 all-reduce.16
  786.8 147.0 all-reduce.18
  945.6 147.1 all-reduce.20
  1104.5 147.3 all-reduce.22
where the time goes:
time: 1290 us; the launch traced here: 1270 us
  waiting for transfers between devices  1160 us (90%)
  matrix products  55.8 us (4%)
  local copies, waits for them, and re-layouts  23.3 us (2%)
  between operations  14.3 us (1%)
  other arithmetic  13.2 us (1%)
    psum x8, waiting for transfers between devices, broadcast(): return lax.psum(kept, axis)  1160 us
    dot_general x8, matrix products, run_sweep(): jnp.dot(jnp.concatenate(masked_columns, axis=1), stacked, precision=precise)  55.8 us
  transfers between devices with their start and end apart: 8, of which 8 were waited for; matrix products, arithmetic and copies ran while one was open for 0% of the time, Pallas kernels for 0%

commit v1 on v0

v1 whole, which is shorter than its diff:
```python
import functools

import jax
import jax.numpy as jnp
from jax import lax
from jax.experimental import pallas as pl
from jax.experimental.pallas import tpu as pltpu
from jax.sharding import PartitionSpec as P

NB = 256
KB = 4
CW = 256
HALF = NB // 2
LAG = 8


def split(value):
    high = value.astype(jnp.bfloat16)
    low = (value - high.astype(jnp.float32)).astype(jnp.bfloat16)
    return high, low


def mm(a, b):
    return jnp.dot(a, b, preferred_element_type=jnp.float32)


def dot_split(a, b):
    return mm(a[0], b[0]) + (mm(a[0], b[1]) + mm(a[1], b[0]))


def dot3(a, b):
    return dot_split(split(a), split(b))


def triangular_inverses(matrices):
    rows = lax.broadcasted_iota(jnp.int32, (NB, NB), 0)
    columns = lax.broadcasted_iota(jnp.int32, (NB, NB), 1)
    same = rows == columns
    ident = jnp.where(same, 1.0, 0.0).astype(jnp.float32)
    scales, offs = [], []
    for matrix in matrices:
        diagonal = jnp.where(same, matrix, 0.0)
        by_row = 1.0 / jnp.sum(diagonal, axis=1, keepdims=True)
        scales.append(1.0 / jnp.sum(diagonal, axis=0, keepdims=True))
        offs.append(jnp.where(same, 0.0, matrix) * by_row)
    count = range(len(matrices))
    inner = (rows // 16) == (columns // 16)
    powers = [jnp.where(inner, -offs[i], 0.0) for i in count]
    results = [ident + powers[i] for i in count]
    reach = 2
    while reach < 16:
        powers = [dot3(powers[i], powers[i]) for i in count]
        results = [results[i] + dot3(results[i], powers[i]) for i in count]
        reach *= 2
    size = 16
    while size < NB:
        pair = ((rows // (2 * size)) == (columns // (2 * size))) & (
            (rows // size) != (columns // size)
        )
        halves = [split(results[i]) for i in count]
        middle = [
            dot_split(split(jnp.where(pair, offs[i], 0.0)), halves[i]) for i in count
        ]
        results = [results[i] - dot_split(halves[i], split(middle[i])) for i in count]
        size *= 2
    return [results[i] * scales[i] for i in count]


def kernel(
    nx, nz, b_ref, l_ref, u_ref, out_ref,
    acc, xbuf, zbuf, lf, uf, lhi, llo, uhi, ulo, diag, inv_hi, inv_lo,
    b_sem, l_sem, u_sem, d_sem, o_sem, recv_f, recv_b, send_f, send_b,
):
    rows = b_ref.shape[0]
    chunks = b_ref.shape[1] // CW
    blocks = chunks * KB
    n = nx * nz
    me = lax.axis_index("row")
    x = me % nx
    z = me // nx
    is_first = me == 0
    is_last = me == n - 1

    def load_b(c):
        return pltpu.make_async_copy(b_ref.at[:, pl.ds(c * CW, CW)], acc.at[c], b_sem.at[c])

    def load_l(k):
        return pltpu.make_async_copy(l_ref.at[:, pl.ds(k * NB, NB)], lf.at[k], l_sem.at[k])

    def load_u(k):
        return pltpu.make_async_copy(u_ref.at[:, pl.ds(k * NB, NB)], uf.at[k], u_sem.at[k])

    def load_d(source, k):
        return pltpu.make_async_copy(
            source.at[pl.ds(k * NB, NB), pl.ds(k * NB, NB)], diag.at[k], d_sem.at[k]
        )

    def store_out(c):
        return pltpu.make_async_copy(acc.at[c], out_ref.at[:, pl.ds(c * CW, CW)], o_sem.at[c])

    @pl.when(is_first)
    def _():
        for k in range(KB):
            load_d(l_ref, k).start()

    @pl.when(is_last)
    def _():
        for k in range(KB):
            load_d(u_ref, k).start()

    load_b(0).start()
    for k in range(KB):
        load_l(k).start()
    for c in range(1, chunks):
        load_b(c).start()
    for k in range(KB):
        load_u(k).start()

    barrier = pltpu.get_barrier_semaphore()
    neighbours = (
        (x >= 1, me - 1),
        (x < nx - 1, me + 1),
        (z >= 1, me - nx),
        (z < nz - 1, me + nx),
    )
    for there, other in neighbours:
        @pl.when(there)
        def _():
            pl.semaphore_signal(
                barrier, inc=1, device_id={"row": other},
                device_id_type=pl.DeviceIdType.MESH,
            )
    peers = sum(jnp.where(there, 1, 0) for there, _ in neighbours)
    pl.semaphore_wait(barrier, peers)

    @pl.when(is_first | is_last)
    def _():
        for k in range(KB):
            load_d(l_ref, k).wait()
        inverses = triangular_inverses([diag[k] for k in range(KB)])
        for k in range(KB):
            high, low = split(inverses[k])
            inv_hi[k] = high
            inv_lo[k] = low

    def children(px, pz, step):
        along_x, along_z = step, step * nx
        tree_a = (
            ((px == 0) & (pz < nz - 1), me + along_z),
            ((pz >= 1) & (px < nx - 1), me + along_x),
            ((pz == 1) & (px >= 1), me - along_z),
        )
        tree_b = (
            ((pz == 0) & (px < nx - 1), me + along_x),
            ((px >= 1) & (pz < nz - 1), me + along_z),
            ((px == 1) & (pz >= 1), me - along_x),
        )
        return (tree_a, tree_b)

    forward_children = children(x, z, 1)
    backward_children = children(nx - 1 - x, nz - 1 - z, -1)

    def remote(buf, recv, send, block, tree, child, other):
        piece = buf.at[block, pl.ds(tree * HALF, HALF), :]
        return pltpu.make_async_remote_copy(
            src_ref=piece, dst_ref=piece,
            send_sem=send.at[block, tree * 3 + child],
            recv_sem=recv.at[block, tree],
            device_id={"row": other}, device_id_type=pl.DeviceIdType.MESH,
        )

    def pass_on(buf, recv, send, block, tree, kids):
        for child in range(3):
            there, other = kids[tree][child]

            @pl.when(there)
            def _():
                remote(buf, recv, send, block, tree, child, other).start()

    def sent(buf, recv, send, block, kids):
        for tree in range(2):
            for child in range(3):
                there, other = kids[tree][child]

                @pl.when(there)
                def _():
                    remote(buf, recv, send, block, tree, child, other).wait_send()

    def sweep_step(block, c, k, owner, buf, recv, send, kids, early, full, high, low, wait_panel):
        @pl.when(owner)
        def _():
            target = acc[c, pl.ds(pl.multiple_of(k * NB, NB), NB), :]
            buf[block] = dot_split((inv_hi[k], inv_lo[k]), split(target))
            for tree in range(2):
                pass_on(buf, recv, send, block, tree, kids)

        @pl.when(jnp.logical_not(owner))
        def _():
            for tree in range(2):
                remote(buf, recv, send, block, tree, 0, me).wait_recv()
                pass_on(buf, recv, send, block, tree, kids)

        @pl.when(early)
        def _():
            wait_panel(k)
            first, second = split(full[k])
            high[k] = first
            low[k] = second

        acc[c] = acc[c] - dot_split((high[k], low[k]), split(buf[block]))

        @pl.when(owner)
        def _():
            acc[c, pl.ds(pl.multiple_of(k * NB, NB), NB), :] = buf[block]

    def event(e, carry):
        @pl.when(e < blocks)
        def _():
            c = e // KB
            k = e % KB

            @pl.when(k == 0)
            def _():
                load_b(c).wait()

            sweep_step(
                e, c, k, is_first, xbuf, recv_f, send_f, forward_children,
                e < KB, lf, lhi, llo, lambda k: load_l(k).wait(),
            )

        @pl.when(e >= LAG)
        def _():
            j = e - LAG
            c = j // KB
            k = KB - 1 - j % KB
            sweep_step(
                j, c, k, is_last, zbuf, recv_b, send_b, backward_children,
                j < KB, uf, uhi, ulo, lambda k: load_u(k).wait(),
            )

            @pl.when(k == 0)
            def _():
                store_out(c).start()

        return carry

    lax.fori_loop(0, blocks + LAG, event, 0)

    def finish(block, carry):
        sent(xbuf, recv_f, send_f, block, forward_children)
        sent(zbuf, recv_b, send_b, block, backward_children)
        return carry

    lax.fori_loop(0, blocks, finish, 0)
    for c in range(chunks):
        store_out(c).wait()


def grid_of(n):
    nx = 2 if n < 32 else 4
    return nx, n // nx


def shards(right_sides, lower_panel, upper_panel):
    rows, width = right_sides.shape
    nx, nz = grid_of(lax.axis_size("row"))
    chunks = width // CW
    blocks = chunks * KB
    f32, bf16 = jnp.float32, jnp.bfloat16
    return pl.pallas_call(
        functools.partial(kernel, nx, nz),
        out_shape=jax.ShapeDtypeStruct((rows, width), f32),
        in_specs=[pl.BlockSpec(memory_space=pl.ANY)] * 3,
        out_specs=pl.BlockSpec(memory_space=pl.ANY),
        scratch_shapes=[
            pltpu.VMEM((chunks, rows, CW), f32),
            pltpu.VMEM((blocks, NB, CW), f32),
            pltpu.VMEM((blocks, NB, CW), f32),
            pltpu.VMEM((KB, rows, NB), f32),
            pltpu.VMEM((KB, rows, NB), f32),
            pltpu.VMEM((KB, rows, NB), bf16),
            pltpu.VMEM((KB, rows, NB), bf16),
            pltpu.VMEM((KB, rows, NB), bf16),
            pltpu.VMEM((KB, rows, NB), bf16),
            pltpu.VMEM((KB, NB, NB), f32),
            pltpu.VMEM((KB, NB, NB), bf16),
            pltpu.VMEM((KB, NB, NB), bf16),
            pltpu.SemaphoreType.DMA((chunks,)),
            pltpu.SemaphoreType.DMA((KB,)),
            pltpu.SemaphoreType.DMA((KB,)),
            pltpu.SemaphoreType.DMA((KB,)),
            pltpu.SemaphoreType.DMA((chunks,)),
            pltpu.SemaphoreType.DMA((blocks, 2)),
            pltpu.SemaphoreType.DMA((blocks, 2)),
            pltpu.SemaphoreType.DMA((blocks, 6)),
            pltpu.SemaphoreType.DMA((blocks, 6)),
        ],
        compiler_params=pltpu.CompilerParams(
            collective_id=0, has_side_effects=True, vmem_limit_bytes=56 * 1024 * 1024
        ),
    )(right_sides, lower_panel, upper_panel)


def solution(mesh):
    placed = (P(("parts", "row"), "col"), P(("parts", "row"), None), P(("parts", "row"), None))
    return jax.shard_map(
        shards, mesh=mesh, in_specs=placed, out_specs=P(("parts", "row"), "col"), check_vma=False
    )
```

time: 1290 us -> 695 us (0.54); the launches traced: 1270 us -> 695 us
  waiting for transfers between devices: 1160 us -> 0 us
  Pallas kernels: 0 us -> 690 us
  matrix products: 55.8 us -> 0 us
  local copies, waits for them, and re-layouts: 23.3 us -> 4.79 us
  between operations: 14.3 us -> 0.01 us
  other arithmetic: 13.2 us -> 0 us
    psum x8 -> x0, waiting for transfers between devices: 1160 us -> none  [broadcast(): return lax.psum(kept, axis)]
    pallas_call x0 -> x1, Pallas kernels: none -> 690 us  [shards(): pl.pallas_call(functools.partial(kernel, nx, nz), out_shape=jax.ShapeDtyp...]
    dot_general x8 -> x0, matrix products: 55.8 us -> none  [run_sweep(): jnp.dot(jnp.concatenate(masked_columns, axis=1), stacked, precision=precise)]
  transfers between devices with their start and end apart: 8 -> 0, of which waited for: 8 -> 0; matrix products, arithmetic and copies ran while one was open for 0% -> 0% of each run, Pallas kernels for 0% -> 0%
where the time goes in v1:
time: 695 us
  Pallas kernels  690 us (99%)
    pallas_call x1, Pallas kernels, shards(): pl.pallas_call(functools.partial(kernel, nx, nz), out_shape=jax.ShapeDtyp...  690 us

profile of v1, /device:TPU:2, one launch (start us, length us, event | category | flops | bytes accessed | tf_op | source)
XLA Modules:
  0.0 694.7 jit_solution(17148236038951147766)
XLA Ops:
  0.0 689.9 %shard_map.37 = f32[1024,1024]{1,0:T(8,128)} custom-call(f32[1024,1024]{1,0:T(8,128)} %b_ref.1, f32[1024,1024]{1,0:T(8,128)} %l_ref.1, f32[1024,1024]{1,0:T(8,128)} %u_ref.1), custom_call_target="tpu_custom_call" | custom-call | tf_op jit(solution)/shard_map/pallas_call | solution.py:270
  689.9 4.8 copy.5

commit v2 on v1

--- a/solution.py
+++ b/solution.py
@@ -11,7 +11,8 @@
 KB = 4
 CW = 256
 HALF = NB // 2
-LAG = 8
+HOP = 2
+SLACK = 0
 
 
 def split(value):
@@ -186,6 +187,12 @@
                 def _():
                     remote(buf, recv, send, block, tree, child, other).wait_send()
 
+    def relay(when, recv, send, buf, kids, tree):
+        @pl.when((when >= 0) & (when < blocks))
+        def _():
+            remote(buf, recv, send, when, tree, 0, me).wait_recv()
+            pass_on(buf, recv, send, when, tree, kids)
+
     def sweep_step(block, c, k, owner, buf, recv, send, kids, early, full, high, low, wait_panel):
         @pl.when(owner)
         def _():
@@ -194,12 +201,6 @@
             for tree in range(2):
                 pass_on(buf, recv, send, block, tree, kids)
 
-        @pl.when(jnp.logical_not(owner))
-        def _():
-            for tree in range(2):
-                remote(buf, recv, send, block, tree, 0, me).wait_recv()
-                pass_on(buf, recv, send, block, tree, kids)
-
         @pl.when(early)
         def _():
             wait_panel(k)
@@ -213,8 +214,32 @@
         def _():
             acc[c, pl.ds(pl.multiple_of(k * NB, NB), NB), :] = buf[block]
 
-    def event(e, carry):
-        @pl.when(e < blocks)
+    def depths(px, pz):
+        depth_a = jnp.where((pz == 0) & (px >= 1), px + 2, px + pz)
+        depth_b = jnp.where((px == 0) & (pz >= 1), pz + 2, px + pz)
+        return HOP * depth_a, HOP * depth_b
+
+    fa, fb = depths(x, z)
+    ba, bb = depths(nx - 1 - x, nz - 1 - z)
+    fc = jnp.maximum(fa, fb)
+    bc = jnp.maximum(ba, bb)
+    lag = KB - 1 + HOP * (nx + nz - 2) + SLACK
+    deepest = HOP * (nx + nz)
+
+    def event(t, carry):
+        @pl.when(jnp.logical_not(is_first))
+        def _():
+            relay(t - fa, recv_f, send_f, xbuf, forward_children, 0)
+            relay(t - fb, recv_f, send_f, xbuf, forward_children, 1)
+
+        @pl.when(jnp.logical_not(is_last))
+        def _():
+            relay(t - lag - ba, recv_b, send_b, zbuf, backward_children, 0)
+            relay(t - lag - bb, recv_b, send_b, zbuf, backward_children, 1)
+
+        e = t - fc
+
+        @pl.when((e >= 0) & (e < blocks))
         def _():
             c = e // KB
             k = e % KB
@@ -228,9 +253,10 @@
                 e < KB, lf, lhi, llo, lambda k: load_l(k).wait(),
             )
 
-        @pl.when(e >= LAG)
-        def _():
-            j = e - LAG
+        j = t - lag - bc
+
+        @pl.when((j >= 0) & (j < blocks))
+        def _():
             c = j // KB
             k = KB - 1 - j % KB
             sweep_step(
@@ -244,7 +270,7 @@
 
         return carry
 
-    lax.fori_loop(0, blocks + LAG, event, 0)
+    lax.fori_loop(0, blocks + lag + deepest + 1, event, 0)
 
     def finish(block, carry):
         sent(xbuf, recv_f, send_f, block, forward_children)

time: 695 us -> 144 us (0.21)
  Pallas kernels: 690 us -> 139 us
    pallas_call x1, Pallas kernels: 690 us -> 139 us  [shards(): pl.pallas_call(functools.partial(kernel, nx, nz), out_shape=jax.ShapeDtyp...]
where the time goes in v2:
time: 144 us; the launch traced here: 143 us
  Pallas kernels  139 us (97%)
  local copies, waits for them, and re-layouts  4.79 us (3%)
    pallas_call x1, Pallas kernels, shards(): pl.pallas_call(functools.partial(kernel, nx, nz), out_shape=jax.ShapeDtyp...  139 us
    unnamed x1, local copies, waits for them, and re-layouts  4.79 us

profile of v2, /device:TPU:2, one launch (start us, length us, event | category | flops | bytes accessed | tf_op | source)
XLA Modules:
  0.0 143.3 jit_solution(12572928363991119753)
XLA Ops:
  0.0 138.5 %shard_map.37 = f32[1024,1024]{1,0:T(8,128)} custom-call(f32[1024,1024]{1,0:T(8,128)} %b_ref.1, f32[1024,1024]{1,0:T(8,128)} %l_ref.1, f32[1024,1024]{1,0:T(8,128)} %u_ref.1), custom_call_target="tpu_custom_call" | custom-call | tf_op jit(solution)/shard_map/pallas_call | solution.py:296
  138.5 4.8 %copy.5 = f32[1024,1024]{1,0:T(8,128)} copy(f32[1024,1024]{1,0:T(8,128)} %shard_map.37) | data formatting | bytes 8388608

commit v3 on v2

--- a/solution.py
+++ b/solution.py
@@ -9,7 +9,7 @@
 
 NB = 256
 KB = 4
-CW = 256
+CW = 128
 HALF = NB // 2
 HOP = 2
 SLACK = 0

time: 144 us -> 140 us (0.972)
  Pallas kernels: 139 us -> 135 us
    pallas_call x1, Pallas kernels: 139 us -> 135 us  [shards(): pl.pallas_call(functools.partial(kernel, nx, nz), out_shape=jax.ShapeDtyp...]
where the time goes in v3:
time: 140 us
  Pallas kernels  135 us (96%)
  local copies, waits for them, and re-layouts  4.79 us (3%)
    pallas_call x1, Pallas kernels, shards(): pl.pallas_call(functools.partial(kernel, nx, nz), out_shape=jax.ShapeDtyp...  135 us
    unnamed x1, local copies, waits for them, and re-layouts  4.79 us

profile of v3, /device:TPU:2, one launch (start us, length us, event | category | flops | bytes accessed | tf_op | source)
XLA Modules:
  0.0 139.6 jit_solution(14601612976475420925)
XLA Ops:
  0.0 134.8 %shard_map.37 = f32[1024,1024]{1,0:T(8,128)} custom-call(f32[1024,1024]{1,0:T(8,128)} %b_ref.1, f32[1024,1024]{1,0:T(8,128)} %l_ref.1, f32[1024,1024]{1,0:T(8,128)} %u_ref.1), custom_call_target="tpu_custom_call" | custom-call | tf_op jit(solution)/shard_map/pallas_call | solution.py:296
  134.8 4.8 %copy.5 = f32[1024,1024]{1,0:T(8,128)} copy(f32[1024,1024]{1,0:T(8,128)} %shard_map.37) | data formatting | bytes 8388608
